TPU v7x, 32 devices: a whole 2x2x4 slice. The times are simulated.
32 devices in a mesh: cls: 4 (over z), ptl: 8 (over y, x, core).
Axes of the slice: x: 2, y: 2, z: 4, core: 2. Of those that a mesh axis runs over, the one named last changes fastest.
Arguments:
- particles: bfloat16 [16384, 64, 128], P(('cls', 'ptl')), may hold values from -6 to 6
- references: bfloat16 [64, 200, 128], P('ptl', 'cls'), may hold values from -0.029907227 to 0.029907227
- best_class: int32 [16384], P(('cls', 'ptl')), may hold values from 0 to 199, as said below
- best_turn: int32 [16384], P(('cls', 'ptl')), may hold values from 0 to 35
Outputs:
- best_score: float32 [16384], P(('cls', 'ptl'))
- new_references: float32 [64, 200, 128], P('ptl', 'cls')
Inputs may be any that keep to these rules, and one draw needn't show every extreme that they name: `best_class`: in each aligned block of 512 rows (the particles of one device), at most 160 classes lie in one class shard, classes k * 50 to (k + 1) * 50 - 1; some class shard receives exactly 160 from every block.
All inputs are finite; a program needn't handle non-finite values.
Results may differ from a plain program's by a relative error of at most 0.0048.
Values may be sent and summed in bfloat16 or wider, within the bound.
A program may use at most 192 MiB of HBM per device.

v0:
```python
import math
import jax
import jax.numpy as jnp
from jax import lax
from jax.sharding import PartitionSpec as P

ROTS = 36
C_DEV = 50
SLOT_CAP = 160


def spectrum_table(angles, freq_count):
    position = jnp.arange(angles, dtype=jnp.int32)
    freq_index = jnp.arange(freq_count, dtype=jnp.int32)
    phases = (
        2.0
        * math.pi
        / angles
        * (position[:, None] * freq_index[None, :] % angles).astype(jnp.float32)
    )
    factor = 1.0 / math.sqrt(angles)
    return (jnp.concatenate([jnp.cos(phases), -jnp.sin(phases)], axis=1) * factor).astype(
        jnp.bfloat16
    )


def rotation_table(freq_count, turns):
    freq_index = jnp.arange(freq_count, dtype=jnp.int32)
    turn_index = jnp.arange(turns, dtype=jnp.int32)
    phases = (
        2.0
        * math.pi
        / turns
        * (freq_index[:, None] * turn_index[None, :] % turns).astype(jnp.float32)
    )
    weight = jnp.where(freq_index == 0, 1.0, 2.0).astype(jnp.float32)[:, None]
    return jnp.stack([weight * jnp.cos(phases), -weight * jnp.sin(phases)]).astype(jnp.bfloat16)


def quarter(panel):
    half_width = panel.shape[-1] // 2
    return jnp.concatenate([panel[..., half_width:], -panel[..., :half_width]], axis=-1)


def rotate_back(spectra, turn_of, turns):
    freq_count = spectra.shape[0]
    half_width = spectra.shape[-1] // 2
    freq_index = jnp.arange(freq_count, dtype=jnp.int32)
    phases = (
        2.0 * math.pi / turns * (freq_index[:, None] * turn_of[None, :] % turns).astype(jnp.float32)
    )
    cosine = jnp.cos(phases)[:, :, None]
    sine_part = jnp.sin(phases)[:, :, None]
    real_part = spectra[..., :half_width].astype(jnp.float32)
    imag_part = spectra[..., half_width:].astype(jnp.float32)
    return jnp.concatenate(
        [real_part * cosine + imag_part * sine_part, imag_part * cosine - real_part * sine_part],
        axis=-1,
    ).astype(jnp.bfloat16)


def polar_spectra(particles, freq_count):
    count_p, cycle_count, angles = particles.shape
    dft_table = spectrum_table(angles, freq_count)
    raw_terms = jnp.einsum("ipa,ak->kip", particles, dft_table, preferred_element_type=jnp.float32)
    spectra = raw_terms.astype(jnp.bfloat16).reshape(2, freq_count, count_p, cycle_count)
    return jnp.transpose(spectra, (1, 2, 0, 3)).reshape(freq_count, count_p, 2 * cycle_count)


def local(particles, references, best_class, best_turn):
    count_p, cycle_count, angles = particles.shape
    freq_count = angles // 2
    spectra = polar_spectra(particles, freq_count)
    turn_table = rotation_table(freq_count, ROTS)
    all_freqs = lax.all_gather(references, "ptl", axis=0, tiled=True)
    group_size = min(count_p, 128)
    panel_part = lax.all_gather(all_freqs, "cls", axis=1, tiled=True)
    class_width = panel_part.shape[1]
    stacked = jnp.concatenate([panel_part, quarter(panel_part)], axis=1)
    maxima = []
    for offset in range(0, count_p, group_size):
        group_rows = spectra[:, offset : offset + group_size]
        cross_terms = jnp.einsum(
            "mik,mck->mic", group_rows, stacked, preferred_element_type=jnp.float32
        ).astype(jnp.bfloat16)
        cross_terms = cross_terms.reshape(freq_count, group_size, 2, class_width)
        scores = jnp.einsum(
            "mijc,jmr->irc", cross_terms, turn_table, preferred_element_type=jnp.float32
        )
        maxima.append(jnp.max(scores, axis=(1, 2)))
    best_score = jnp.concatenate(maxima)
    aligned = rotate_back(spectra, best_turn, ROTS)
    owners = lax.axis_size("cls")
    peer_count = lax.axis_size("ptl")
    slot_cap = SLOT_CAP
    owner_of = best_class // C_DEV
    local_class = best_class - owner_of * C_DEV
    owner_hits = (owner_of[:, None] == jnp.arange(owners, dtype=jnp.int32)[None, :]).astype(
        jnp.int32
    )
    slot_rank = jnp.sum((jnp.cumsum(owner_hits, axis=0) - owner_hits) * owner_hits, axis=1)
    slot_index = owner_of * slot_cap + slot_rank
    outgoing = jnp.zeros((freq_count, owners * slot_cap, 2 * cycle_count), jnp.bfloat16)
    outgoing = (
        outgoing.at[:, slot_index, :]
        .set(aligned)
        .reshape(freq_count, owners, slot_cap, 2 * cycle_count)
    )
    labels = (
        jnp.full((owners * slot_cap,), -1.0, jnp.bfloat16)
        .at[slot_index]
        .set(local_class.astype(jnp.bfloat16))
    )
    labels = jnp.broadcast_to(labels.reshape(1, owners, slot_cap), (peer_count, owners, slot_cap))
    arrived, arrived_labels = (
        lax.all_to_all(
            lax.all_to_all(outgoing, "cls", split_axis=1, concat_axis=1, tiled=True),
            "ptl",
            split_axis=0,
            concat_axis=2,
            tiled=True,
        ),
        lax.all_to_all(
            lax.all_to_all(labels, "cls", split_axis=1, concat_axis=1, tiled=True),
            "ptl",
            split_axis=0,
            concat_axis=2,
            tiled=True,
        ),
    )
    arrived_rows = arrived.reshape(arrived.shape[0], -1, 2 * cycle_count)
    class_marks = jnp.arange(C_DEV, dtype=jnp.float32).astype(jnp.bfloat16)
    member = (arrived_labels.reshape(1, -1) == class_marks[:, None]).astype(jnp.bfloat16)
    totals = jnp.einsum("cs,msk->mck", member, arrived_rows, preferred_element_type=jnp.float32)
    counts = jnp.sum(member.astype(jnp.float32), axis=1)
    new_references = totals / (counts + 1.0)[None, :, None]
    return (best_score, new_references)


def solution(mesh):
    return jax.shard_map(
        local,
        mesh=mesh,
        in_specs=(
            P(("cls", "ptl"), None, None),
            P("ptl", "cls", None),
            P(("cls", "ptl")),
            P(("cls", "ptl")),
        ),
        out_specs=(P(("cls", "ptl")), P("ptl", "cls", None)),
        check_vma=False,
    )
```

profile of v0, /device:TPU:0, one launch (start us, length us, event | category | flops | bytes accessed | tf_op | source)
XLA Modules:
  0.0 620.9 jit_solution(3257332240550867480)
XLA Ops:
  7.2 0.7 subtract_convert_fusion
  7.9 1.2 reduce-window.6
  9.1 0.2 slice_reduce_fusion
  9.3 0.2 reduce-window.9
  9.5 0.1 add_bitcast_fusion
  9.6 3.8 scatter_custom_fusion.1
  13.4 0.1 broadcast_in_dim.23
  13.5 0.6 broadcast_in_dim.44
  14.1 6.5 %all-to-all-start.2 = ((bf16[8,4,160]{2,0,1:T(8,128)(2,1)}), bf16[8,4,160]{2,0,1:T(8,128)(2,1)S(1)}, u32[]{:S(2)}, u32[]{:S(2)}) async-start(bf16[8,4,160]{2,0,1:T(8,128)(2,1)} %broadcast_in_dim.44), calls=%async_computation.2 | async-start | bytes 32768 | tf_op jit(solution)/shard_map/all_to_all | solution.py:124
  20.6 0.1 sine_negate_fusion
  20.8 25.2 %fusion.6 = bf16[128,512,64]{1,0,2:T(8,128)(2,1)} fusion(bf16[512,64,128]{2,1,0:T(8,128)(2,1)} %param.4, f32[128,64]{0,1:T(8,128)S(1)} %get-tuple-element.18, f32[128,64]{0,1:T(8,128)S(1)} %get-tuple-element.19), kind=kOutput, calls=%fused_computation.17 | convolution fusion | flops 1077985280 | bytes 16842752 | tf_op jit(solution)/shard_map/ipa,ak->kip/dot_general | solution.py:65
  46.0 0.0 copy-start.1
  46.0 11.4 %copy.50 = bf16[2,64,512,64]{2,3,0,1:T(8,128)(2,1)} copy(bf16[2,64,512,64]{2,1,0,3:T(8,128)(2,1)} %bitcast.76) | data formatting | bytes 16777216 | tf_op jit(solution)/shard_map/reshape | solution.py:66
  57.4 0.0 copy-done.1
  57.4 0.5 fusion.37
  57.9 7.7 %fusion.1 = (bf16[64,512,64]{1,2,0:T(8,128)(2,1)}, bf16[64,512,64]{1,2,0:T(8,128)(2,1)}) fusion(f32[64,512]{1,0:T(8,128)S(1)} %get-tuple-element.17, f32[64,512]{1,0:T(8,128)S(1)} %get-tuple-element.16, bf16[64,512,128]{1,2,0:T(8,128)(2,1)} %bitcast.69), kind=kLoop, calls=%fused_computation.7 | loop fusion | flops 20971520 | bytes 17039360 | tf_op jit(solution)/shard_map/convert
  65.6 7.7 %maximum_bitcast_fusion = bf16[512,64,128]{0,2,1:T(8,128)(2,1)} fusion(bf16[64,512,64]{1,2,0:T(8,128)(2,1)} %get-tuple-element.13, bf16[64,512,64]{1,2,0:T(8,128)(2,1)} %get-tuple-element.12), kind=kLoop, calls=%fused_computation.10 | loop fusion | flops 16777216 | bytes 16777216 | tf_op jit(solution)/shard_map/concatenate | solution.py:56
  73.3 12.0 %copy.62 = bf16[512,64,128]{2,1,0:T(8,128)(2,1)} copy(bf16[512,64,128]{0,2,1:T(8,128)(2,1)} %maximum_bitcast_fusion) | data formatting | bytes 16777216 | tf_op jit(solution)/shard_map/concatenate | solution.py:56
  85.3 6.7 %broadcast_in_dim.20 = bf16[64,640,128]{2,0,1:T(8,128)(2,1)} broadcast(bf16[]{:T(256)} %constant.66.clone.1), dimensions={} | broadcast | bytes 10485762 | tf_op jit(solution)/shard_map/broadcast_in_dim | solution.py:103
  92.0 66.3 %scatter_fusion = bf16[64,640,128]{2,0,1:T(8,128)(2,1)} fusion(bf16[64,640,128]{2,0,1:T(8,128)(2,1)} %broadcast_in_dim.20, s32[512]{0:T(512)S(1)} %compare_select_fusion, bf16[512,64,128]{2,1,0:T(8,128)(2,1)} %copy.62), kind=kCustom, calls=%fused_computation | custom fusion | bytes 25167872 | tf_op jit(solution)/shard_map/scatter | solution.py:106
  158.3 14.6 %copy.63 = bf16[64,4,160,128]{3,2,0,1:T(8,128)(2,1)} copy(bf16[64,4,160,128]{3,0,2,1:T(8,128)(2,1)} %bitcast.67) | data formatting | bytes 20971520 | tf_op jit(solution)/shard_map/reshape | solution.py:107
  172.9 0.0 copy-start
  172.9 0.0 all-to-all-done.2
  172.9 6.1 all-to-all-start
  179.0 0.0 all-gather.2.cloned.1.call-start
  179.1 0.0 copy-done
  179.1 12.0 %all_gather.6 = bf16[64,50,128]{2,0,1:T(8,128)(2,1)} all-gather(bf16[8,50,128]{2,0,1:T(8,128)(2,1)S(1)} %copy-done), channel_id=1, replica_groups=mesh['cls'=4,'ptl'=8] {'ptl'}, dimensions={0}, use_global_device_ids=true | all-gather | bytes 921600 | tf_op jit(solution)/shard_map/all_gather | solution.py:75
  191.1 0.0 all-gather.2.cloned.1.call-update
  191.1 0.6 copy.66
  191.7 268.0 %all-to-all-done = bf16[64,4,160,128]{3,2,0,1:T(8,128)(2,1)} async-done(((bf16[64,4,160,128]{3,2,0,1:T(8,128)(2,1)}), bf16[64,4,160,128]{3,2,0,1:T(8,128)(2,1)}, u32[]{:S(2)}, u32[]{:S(2)}) %all-to-all-start) | async-done | bytes 10485792 | tf_op jit(solution)/shard_map/all_to_all | solution.py:117
  459.7 3.8 all-to-all-start.3
  463.5 11.1 %copy.64 = bf16[64,4,160,128]{3,2,1,0:T(8,128)(2,1)} copy(bf16[64,4,160,128]{3,2,0,1:T(8,128)(2,1)} %all-to-all-done) | data formatting | bytes 20971520 | tf_op jit(solution)/shard_map/all_to_all | solution.py:117
  474.5 0.0 all-to-all-done.3
  474.5 5.1 all-to-all-start.1
  479.7 0.1 multiply_convert_fusion
  479.9 0.1 eq.68
  480.0 0.3 convert_reduce_fusion
  480.3 0.0 all-gather.2.cloned.1.call-done
  480.3 0.0 slice-start
  480.3 4.2 copy.54
  484.5 0.0 slice-start.1
  484.5 3.0 fusion.65
  487.5 0.0 slice-done
  487.5 0.0 slice-done.1
  487.5 7.1 %convolution_convert_fusion.3 = bf16[64,128,400]{1,2,0:T(8,128)(2,1)} fusion(bf16[64,512,128]{1,2,0:T(8,128)(2,1)S(1)} %bitcast.72, bf16[64,200,64]{2,1,0:T(8,128)(2,1)} %get-tuple-element.15, bf16[64,200,64]{2,1,0:T(8,128)(2,1)S(1)} %get-tuple-element.14, bf16[64,200,128]{2,1,0:T(8,128)(2,1)S(1)} %copy.54), kind=kOutput, calls=%fused_computation.16 | convolution fusion | flops 861798400 | bytes 16842752 | tf_op jit(solution)/shard_map/mik,mck->mic/dot_general | solution.py:83
  494.6 4.5 bitcast_reduce_fusion.3
  499.1 7.1 %convolution_convert_fusion.2 = bf16[64,128,400]{1,2,0:T(8,128)(2,1)} fusion(bf16[64,512,128]{1,2,0:T(8,128)(2,1)S(1)} %bitcast.73, bf16[64,200,64]{2,1,0:T(8,128)(2,1)} %get-tuple-element.15, bf16[64,200,64]{2,1,0:T(8,128)(2,1)S(1)} %get-tuple-element.14, bf16[64,200,128]{2,1,0:T(8,128)(2,1)S(1)} %copy.54), kind=kOutput, calls=%fused_computation.15 | convolution fusion | flops 861798400 | bytes 16842752 | tf_op jit(solution)/shard_map/mik,mck->mic/dot_general | solution.py:83
  506.1 4.5 bitcast_reduce_fusion.2
  510.6 7.3 %convolution_convert_fusion.1 = bf16[64,128,400]{1,2,0:T(8,128)(2,1)} fusion(bf16[64,512,128]{1,2,0:T(8,128)(2,1)S(1)} %bitcast.74, bf16[64,200,64]{2,1,0:T(8,128)(2,1)} %get-tuple-element.15, bf16[64,200,64]{2,1,0:T(8,128)(2,1)S(1)} %get-tuple-element.14, bf16[64,200,128]{2,1,0:T(8,128)(2,1)S(1)} %copy.54), kind=kOutput, calls=%fused_computation.14 | convolution fusion | flops 861798400 | bytes 16842752 | tf_op jit(solution)/shard_map/mik,mck->mic/dot_general | solution.py:83
  517.9 4.5 bitcast_reduce_fusion.1
  522.4 7.1 %convolution_convert_fusion = bf16[64,128,400]{1,2,0:T(8,128)(2,1)} fusion(bf16[64,512,128]{1,2,0:T(8,128)(2,1)S(1)} %bitcast.75, bf16[64,200,64]{2,1,0:T(8,128)(2,1)} %get-tuple-element.15, bf16[64,200,64]{2,1,0:T(8,128)(2,1)S(1)} %get-tuple-element.14, bf16[64,200,128]{2,1,0:T(8,128)(2,1)S(1)} %copy.54), kind=kOutput, calls=%fused_computation.13 | convolution fusion | flops 861798400 | bytes 16842752 | tf_op jit(solution)/shard_map/mik,mck->mic/dot_general | solution.py:83
  529.5 4.5 bitcast_reduce_fusion
  534.0 0.6 pad_maximum_fusion
  534.6 61.7 %all-to-all-done.1 = bf16[64,4,160,128]{3,2,1,0:T(8,128)(2,1)} async-done(((bf16[64,4,160,128]{3,2,1,0:T(8,128)(2,1)}), bf16[64,4,160,128]{3,2,1,0:T(8,128)(2,1)}, u32[]{:S(2)}, u32[]{:S(2)}) %all-to-all-start.1) | async-done | bytes 10485792 | tf_op jit(solution)/shard_map/all_to_all | solution.py:116
  596.2 10.7 %copy.65 = bf16[8,4,8,160,128]{4,3,2,1,0:T(8,128)(2,1)} copy(bf16[8,4,8,160,128]{4,3,1,0,2:T(8,128)(2,1)} %bitcast.23) | data formatting | bytes 20971520 | tf_op jit(solution)/shard_map/all_to_all | solution.py:116
  606.9 6.0 fusion.29
  612.9 0.7 copy.68
  (9 shorter events, 0.1 us)
Async XLA Ops:
  14.1 158.8 %all-to-all-start.2 = ((bf16[8,4,160]{2,0,1:T(8,128)(2,1)}), bf16[8,4,160]{2,0,1:T(8,128)(2,1)S(1)}, u32[]{:S(2)}, u32[]{:S(2)}) async-start(bf16[8,4,160]{2,0,1:T(8,128)(2,1)} %broadcast_in_dim.44), calls=%async_computation.2 | async-start | bytes 32768 | tf_op jit(solution)/shard_map/all_to_all | solution.py:124
  46.0 11.4 %copy-start.1 = (s32[512]{0:T(512)S(1)}, s32[512]{0:T(512)}, u32[]{:S(2)}) copy-start(s32[512]{0:T(512)} %param.7) | copy-start | bytes 6148
  172.9 6.2 copy-start
  172.9 286.8 %all-to-all-start = ((bf16[64,4,160,128]{3,2,0,1:T(8,128)(2,1)}), bf16[64,4,160,128]{3,2,0,1:T(8,128)(2,1)}, u32[]{:S(2)}, u32[]{:S(2)}) async-start(bf16[64,4,160,128]{3,2,0,1:T(8,128)(2,1)} %copy.63), calls=%async_computation | async-start | bytes 20971520 | tf_op jit(solution)/shard_map/all_to_all | solution.py:117
  179.0 301.3 %all-gather.2.cloned.1.call-start = ((), (), s32[]{:S(2)}) async-start(), calls=%async_computation.4 | async-start | bytes 4096000 | tf_op jit(solution)/shard_map/all_gather | solution.py:77
  459.7 14.8 %all-to-all-start.3 = ((bf16[8,4,160]{2,1,0:T(4,128)(2,1)}), bf16[8,4,160]{2,1,0:T(4,128)(2,1)S(1)}, u32[]{:S(2)}, u32[]{:S(2)}) async-start(bf16[8,4,160]{2,1,0:T(4,128)(2,1)} %copy.66), calls=%async_computation.3 | async-start | bytes 32768 | tf_op jit(solution)/shard_map/all_to_all | solution.py:123
  474.5 121.7 %all-to-all-start.1 = ((bf16[64,4,160,128]{3,2,1,0:T(8,128)(2,1)}), bf16[64,4,160,128]{3,2,1,0:T(8,128)(2,1)}, u32[]{:S(2)}, u32[]{:S(2)}) async-start(bf16[64,4,160,128]{3,2,1,0:T(8,128)(2,1)} %copy.64), calls=%async_computation.1 | async-start | bytes 20971520 | tf_op jit(solution)/shard_map/all_to_all | solution.py:116
  480.3 7.2 %slice-start = ((s8[8388608]{0:T(1024)(128)(4,1)}), s8[4194304]{0:T(1024)(128)(4,1)S(1)}, s32[]{:S(2)}) async-start(s8[8388608]{0:T(1024)(128)(4,1)} %bitcast.70), calls=%async_computation.5 | async-start | bytes 8388608
  484.5 3.0 slice-start.1
Sparse Core Ops, SparseCore 0:
  191.2 127.6 all-gather.1
where the time goes:
time: 626 us; the launch traced here: 621 us
  waiting for transfers between devices  330 us (53%)
  local copies, waits for them, and re-layouts  143 us (23%)
  matrix products  77.6 us (12%)
  other arithmetic  22.3 us (4%)
  starting transfers between devices  21.6 us (3%)
  between operations  14.6 us (2%)
  blocking collectives  12 us (2%)
    all_to_all x1, waiting for transfers between devices, local(): lax.all_to_all(outgoing, 'cls', split_axis=1, concat_axis=1, tiled=True)  268 us
    scatter x1, local copies, waits for them, and re-layouts, local(): outgoing = outgoing.at[:, slot_index, :].set(aligned).reshape(freq_count,...  66.3 us
    all_to_all x1, waiting for transfers between devices, local(): lax.all_to_all(lax.all_to_all(outgoing, 'cls', split_axis=1, concat_axis=...  61.7 us
    dot_general x4, matrix products, local(): jnp.einsum('mik,mck->mic', group_rows, stacked, preferred_element_type=jn...  28.5 us
    dot_general x1, matrix products, polar_spectra(): jnp.einsum('ipa,ak->kip', particles, dft_table, preferred_element_type=jn...  25.2 us
    dot_general x4, matrix products, local(): jnp.einsum('mijc,jmr->irc', cross_terms, turn_table, preferred_element_ty...  18 us
    reshape x1, local copies, waits for them, and re-layouts, local(): outgoing = outgoing.at[:, slot_index, :].set(aligned).reshape(freq_count,...  14.6 us
  transfers between devices with their start and end apart: 5, of which 2 were waited for; matrix products, arithmetic and copies ran while one was open for 35% of the time, Pallas kernels for 0%

commit v1 on v0

--- a/solution.py
+++ b/solution.py
@@ -113,12 +113,20 @@
     )
     labels = jnp.broadcast_to(labels.reshape(1, owners, slot_cap), (peer_count, owners, slot_cap))
     arrived, arrived_labels = (
-        lax.all_to_all(
-            lax.all_to_all(outgoing, "cls", split_axis=1, concat_axis=1, tiled=True),
-            "ptl",
-            split_axis=0,
-            concat_axis=2,
-            tiled=True,
+        jnp.concatenate(
+            lax.all_to_all(
+                jnp.stack(
+                    jnp.split(
+                        lax.all_to_all(outgoing, "cls", split_axis=1, concat_axis=1, tiled=True),
+                        lax.axis_size("ptl"),
+                        axis=0,
+                    )
+                ),
+                "ptl",
+                0,
+                0,
+            ),
+            axis=2,
         ),
         lax.all_to_all(
             lax.all_to_all(labels, "cls", split_axis=1, concat_axis=1, tiled=True),

time: 626 us -> 646 us (1.032)
  local copies, waits for them, and re-layouts: 143 us -> 163 us
    all_to_all x2 -> x0, local copies, waits for them, and re-layouts: 21.7 us -> none  [the longest x1 11.1 us: local(): lax.all_to_all(outgoing, 'cls', split_axis=1, concat_axis=1, tiled=True)]
    unnamed x9 -> x16, local copies, waits for them, and re-layouts: 0.74 us -> 18.4 us
    another operation x0 -> x2, local copies, waits for them, and re-layouts: none -> 13.4 us  [local(): jnp.stack(jnp.split(lax.all_to_all(outgoing, 'cls', split_axis=1, concat_...]
    reshape x0 -> x1, local copies, waits for them, and re-layouts: none -> 10.7 us  [local(): jnp.concatenate(lax.all_to_all(jnp.stack(jnp.split(lax.all_to_all(outgoin...]
  transfers between devices with their start and end apart: 5 -> 5, of which waited for: 2 -> 2; matrix products, arithmetic and copies ran while one was open for 35% -> 37% of each run, Pallas kernels for 0% -> 0%
where the time goes in v1:
time: 646 us; the launch traced here: 641 us
  waiting for transfers between devices  330 us (51%)
  local copies, waits for them, and re-layouts  163 us (25%)
  matrix products  77.4 us (12%)
  other arithmetic  22.6 us (3%)
  starting transfers between devices  21.8 us (3%)
  between operations  14.4 us (2%)
  blocking collectives  12 us (2%)
    all_to_all x1, waiting for transfers between devices, local(): lax.all_to_all(outgoing, 'cls', split_axis=1, concat_axis=1, tiled=True)  268 us
    scatter x1, local copies, waits for them, and re-layouts, local(): outgoing = outgoing.at[:, slot_index, :].set(aligned).reshape(freq_count,...  66.3 us
    all_to_all x1, waiting for transfers between devices, local(): lax.all_to_all(jnp.stack(jnp.split(lax.all_to_all(outgoing, 'cls', split_...  61.6 us
    dot_general x4, matrix products, local(): jnp.einsum('mik,mck->mic', group_rows, stacked, preferred_element_type=jn...  28.5 us
    dot_general x1, matrix products, polar_spectra(): jnp.einsum('ipa,ak->kip', particles, dft_table, preferred_element_type=jn...  25 us
    unnamed x16, local copies, waits for them, and re-layouts  18.4 us
    dot_general x4, matrix products, local(): jnp.einsum('mijc,jmr->irc', cross_terms, turn_table, preferred_element_ty...  18 us
    reshape x1, local copies, waits for them, and re-layouts, local(): outgoing = outgoing.at[:, slot_index, :].set(aligned).reshape(freq_count,...  14.6 us
  transfers between devices with their start and end apart: 5, of which 2 were waited for; matrix products, arithmetic and copies ran while one was open for 37% of the time, Pallas kernels for 0%

profile of v1, /device:TPU:0, one launch (start us, length us, event | category | flops | bytes accessed | tf_op | source)
XLA Modules:
  0.0 640.9 jit_solution(10581008678109507693)
XLA Ops:
  7.2 0.7 subtract_convert_fusion
  7.9 1.2 reduce-window.6
  9.1 0.2 slice_reduce_fusion
  9.3 0.2 reduce-window.9
  9.5 0.1 add_bitcast_fusion
  9.6 3.8 scatter_custom_fusion.1
  13.4 0.1 broadcast_in_dim.23
  13.5 0.6 broadcast_in_dim.44
  14.1 6.8 %all-to-all-start.2 = ((bf16[8,4,160]{2,0,1:T(8,128)(2,1)}), bf16[8,4,160]{2,0,1:T(8,128)(2,1)S(1)}, u32[]{:S(2)}, u32[]{:S(2)}) async-start(bf16[8,4,160]{2,0,1:T(8,128)(2,1)} %broadcast_in_dim.44), calls=%async_computation.2 | async-start | bytes 32768 | tf_op jit(solution)/shard_map/all_to_all | solution.py:132
  20.9 0.1 sine_negate_fusion
  21.0 25.0 %fusion.6 = bf16[128,512,64]{1,0,2:T(8,128)(2,1)} fusion(bf16[512,64,128]{2,1,0:T(8,128)(2,1)} %param.4, f32[128,64]{0,1:T(8,128)S(1)} %get-tuple-element.18, f32[128,64]{0,1:T(8,128)S(1)} %get-tuple-element.19), kind=kOutput, calls=%fused_computation.17 | convolution fusion | flops 1077985280 | bytes 16842752 | tf_op jit(solution)/shard_map/ipa,ak->kip/dot_general | solution.py:65
  46.0 0.0 copy-start.1
  46.0 11.4 %copy.64 = bf16[2,64,512,64]{2,3,0,1:T(8,128)(2,1)} copy(bf16[2,64,512,64]{2,1,0,3:T(8,128)(2,1)} %bitcast.106) | data formatting | bytes 16777216 | tf_op jit(solution)/shard_map/reshape | solution.py:66
  57.4 0.0 copy-done.1
  57.4 0.5 fusion.45
  57.9 7.9 %fusion.1 = (bf16[64,512,64]{1,2,0:T(8,128)(2,1)}, bf16[64,512,64]{1,2,0:T(8,128)(2,1)}) fusion(f32[64,512]{1,0:T(8,128)S(1)} %get-tuple-element.17, f32[64,512]{1,0:T(8,128)S(1)} %get-tuple-element.16, bf16[64,512,128]{1,2,0:T(8,128)(2,1)} %bitcast.99), kind=kLoop, calls=%fused_computation.7 | loop fusion | flops 20971520 | bytes 17039360 | tf_op jit(solution)/shard_map/convert
  65.8 7.7 %maximum_bitcast_fusion = bf16[512,64,128]{0,2,1:T(8,128)(2,1)} fusion(bf16[64,512,64]{1,2,0:T(8,128)(2,1)} %get-tuple-element.13, bf16[64,512,64]{1,2,0:T(8,128)(2,1)} %get-tuple-element.12), kind=kLoop, calls=%fused_computation.10 | loop fusion | flops 16777216 | bytes 16777216 | tf_op jit(solution)/shard_map/concatenate | solution.py:56
  73.5 12.0 %copy.76 = bf16[512,64,128]{2,1,0:T(8,128)(2,1)} copy(bf16[512,64,128]{0,2,1:T(8,128)(2,1)} %maximum_bitcast_fusion) | data formatting | bytes 16777216 | tf_op jit(solution)/shard_map/concatenate | solution.py:56
  85.5 6.7 %broadcast_in_dim.20 = bf16[64,640,128]{2,0,1:T(8,128)(2,1)} broadcast(bf16[]{:T(256)} %constant.66.clone.1), dimensions={} | broadcast | bytes 10485762 | tf_op jit(solution)/shard_map/broadcast_in_dim | solution.py:103
  92.2 66.3 %scatter_fusion = bf16[64,640,128]{2,0,1:T(8,128)(2,1)} fusion(bf16[64,640,128]{2,0,1:T(8,128)(2,1)} %broadcast_in_dim.20, s32[512]{0:T(512)S(1)} %compare_select_fusion, bf16[512,64,128]{2,1,0:T(8,128)(2,1)} %copy.76), kind=kCustom, calls=%fused_computation | custom fusion | bytes 25167872 | tf_op jit(solution)/shard_map/scatter | solution.py:106
  158.5 14.6 %copy.77 = bf16[64,4,160,128]{3,2,0,1:T(8,128)(2,1)} copy(bf16[64,4,160,128]{3,0,2,1:T(8,128)(2,1)} %bitcast.97) | data formatting | bytes 20971520 | tf_op jit(solution)/shard_map/reshape | solution.py:107
  173.1 0.0 all-to-all-done.2
  173.1 6.1 all-to-all-start
  179.2 0.0 all-gather.2.cloned.1.call-start
  179.3 0.0 copy-done
  179.3 12.0 %all_gather.6 = bf16[64,50,128]{2,0,1:T(8,128)(2,1)} all-gather(bf16[8,50,128]{2,0,1:T(8,128)(2,1)S(1)} %copy-done), channel_id=1, replica_groups=mesh['cls'=4,'ptl'=8] {'ptl'}, dimensions={0}, use_global_device_ids=true | all-gather | bytes 921600 | tf_op jit(solution)/shard_map/all_gather | solution.py:75
  191.2 0.0 all-gather.2.cloned.1.call-update
  191.3 0.6 copy.80
  191.9 268.0 %all-to-all-done = bf16[64,4,160,128]{3,2,0,1:T(8,128)(2,1)} async-done(((bf16[64,4,160,128]{3,2,0,1:T(8,128)(2,1)}), bf16[64,4,160,128]{3,2,0,1:T(8,128)(2,1)}, u32[]{:S(2)}, u32[]{:S(2)}) %all-to-all-start) | async-done | bytes 10485792 | tf_op jit(solution)/shard_map/all_to_all | solution.py:120
  459.9 3.8 all-to-all-start.3
  463.7 2.5 fusion.36
  466.2 2.5 fusion.35
  468.7 2.5 fusion.34
  471.2 2.6 fusion.33
  473.8 2.5 fusion.32
  476.3 2.5 fusion.31
  478.8 2.6 fusion.30
  481.4 2.5 fusion.29
  483.9 10.9 %copy.78 = bf16[8,8,4,160,128]{4,3,2,1,0:T(8,128)(2,1)} copy(bf16[8,8,4,160,128]{4,3,1,2,0:T(8,128)(2,1)} %fusion.29) | data formatting | bytes 20971520 | tf_op jit(solution)/shard_map/stack | solution.py:118
  494.8 0.0 all-to-all-done.3
  494.8 5.1 all-to-all-start.1
  500.0 0.1 multiply_convert_fusion
  500.1 0.1 eq.68
  500.2 0.3 convert_reduce_fusion
  500.5 0.0 all-gather.2.cloned.1.call-done
  500.6 0.0 slice-start
  500.6 4.2 copy.68
  504.8 0.0 slice-start.1
  504.8 3.1 fusion.73
  507.9 0.0 slice-done
  507.9 0.0 slice-done.1
  507.9 7.1 %convolution_convert_fusion = bf16[64,128,400]{1,2,0:T(8,128)(2,1)} fusion(bf16[64,512,128]{1,2,0:T(8,128)(2,1)S(1)} %bitcast.102, bf16[64,200,64]{2,1,0:T(8,128)(2,1)} %get-tuple-element.15, bf16[64,200,64]{2,1,0:T(8,128)(2,1)S(1)} %get-tuple-element.14, bf16[64,200,128]{2,1,0:T(8,128)(2,1)S(1)} %copy.68), kind=kOutput, calls=%fused_computation.13 | convolution fusion | flops 861798400 | bytes 16842752 | tf_op jit(solution)/shard_map/mik,mck->mic/dot_general | solution.py:83
  514.9 4.5 bitcast_reduce_fusion
  519.4 7.1 %convolution_convert_fusion.1 = bf16[64,128,400]{1,2,0:T(8,128)(2,1)} fusion(bf16[64,512,128]{1,2,0:T(8,128)(2,1)S(1)} %bitcast.103, bf16[64,200,64]{2,1,0:T(8,128)(2,1)} %get-tuple-element.15, bf16[64,200,64]{2,1,0:T(8,128)(2,1)S(1)} %get-tuple-element.14, bf16[64,200,128]{2,1,0:T(8,128)(2,1)S(1)} %copy.68), kind=kOutput, calls=%fused_computation.14 | convolution fusion | flops 861798400 | bytes 16842752 | tf_op jit(solution)/shard_map/mik,mck->mic/dot_general | solution.py:83
  526.5 4.5 bitcast_reduce_fusion.1
  531.0 7.3 %convolution_convert_fusion.2 = bf16[64,128,400]{1,2,0:T(8,128)(2,1)} fusion(bf16[64,512,128]{1,2,0:T(8,128)(2,1)S(1)} %bitcast.104, bf16[64,200,64]{2,1,0:T(8,128)(2,1)} %get-tuple-element.15, bf16[64,200,64]{2,1,0:T(8,128)(2,1)S(1)} %get-tuple-element.14, bf16[64,200,128]{2,1,0:T(8,128)(2,1)S(1)} %copy.68), kind=kOutput, calls=%fused_computation.15 | convolution fusion | flops 861798400 | bytes 16842752 | tf_op jit(solution)/shard_map/mik,mck->mic/dot_general | solution.py:83
  538.3 4.5 bitcast_reduce_fusion.2
  542.8 7.1 %convolution_convert_fusion.3 = bf16[64,128,400]{1,2,0:T(8,128)(2,1)} fusion(bf16[64,512,128]{1,2,0:T(8,128)(2,1)S(1)} %bitcast.105, bf16[64,200,64]{2,1,0:T(8,128)(2,1)} %get-tuple-element.15, bf16[64,200,64]{2,1,0:T(8,128)(2,1)S(1)} %get-tuple-element.14, bf16[64,200,128]{2,1,0:T(8,128)(2,1)S(1)} %copy.68), kind=kOutput, calls=%fused_computation.16 | convolution fusion | flops 861798400 | bytes 16842752 | tf_op jit(solution)/shard_map/mik,mck->mic/dot_general | solution.py:83
  549.8 4.5 bitcast_reduce_fusion.3
  554.3 0.6 pad_maximum_fusion
  554.9 61.6 %all-to-all-done.1 = bf16[8,8,4,160,128]{4,3,2,1,0:T(8,128)(2,1)} async-done(((bf16[8,8,4,160,128]{4,3,2,1,0:T(8,128)(2,1)}), bf16[8,8,4,160,128]{4,3,2,1,0:T(8,128)(2,1)}, u32[]{:S(2)}, u32[]{:S(2)}) %all-to-all-start.1) | async-done | bytes 10485792 | tf_op jit(solution)/shard_map/all_to_all | solution.py:117
  616.5 10.7 %copy.79 = bf16[8,4,8,160,128]{4,3,2,1,0:T(8,128)(2,1)} copy(bf16[8,4,8,160,128]{4,3,1,0,2:T(8,128)(2,1)} %bitcast.30) | data formatting | bytes 20971520 | tf_op jit(solution)/shard_map/reshape | solution.py:116
  627.2 6.0 fusion.37
  633.1 0.7 copy.82
  (10 shorter events, 0.1 us)
Async XLA Ops:
  14.1 159.0 %all-to-all-start.2 = ((bf16[8,4,160]{2,0,1:T(8,128)(2,1)}), bf16[8,4,160]{2,0,1:T(8,128)(2,1)S(1)}, u32[]{:S(2)}, u32[]{:S(2)}) async-start(bf16[8,4,160]{2,0,1:T(8,128)(2,1)} %broadcast_in_dim.44), calls=%async_computation.2 | async-start | bytes 32768 | tf_op jit(solution)/shard_map/all_to_all | solution.py:132
  46.0 11.4 %copy-start.1 = (s32[512]{0:T(512)S(1)}, s32[512]{0:T(512)}, u32[]{:S(2)}) copy-start(s32[512]{0:T(512)} %param.7) | copy-start | bytes 6148
  173.1 6.2 copy-start
  173.1 286.8 %all-to-all-start = ((bf16[64,4,160,128]{3,2,0,1:T(8,128)(2,1)}), bf16[64,4,160,128]{3,2,0,1:T(8,128)(2,1)}, u32[]{:S(2)}, u32[]{:S(2)}) async-start(bf16[64,4,160,128]{3,2,0,1:T(8,128)(2,1)} %copy.77), calls=%async_computation | async-start | bytes 20971520 | tf_op jit(solution)/shard_map/all_to_all | solution.py:120
  179.2 321.3 %all-gather.2.cloned.1.call-start = ((), (), s32[]{:S(2)}) async-start(), calls=%async_computation.4 | async-start | bytes 4096000 | tf_op jit(solution)/shard_map/all_gather | solution.py:77
  459.9 34.9 %all-to-all-start.3 = ((bf16[8,4,160]{2,1,0:T(4,128)(2,1)}), bf16[8,4,160]{2,1,0:T(4,128)(2,1)S(1)}, u32[]{:S(2)}, u32[]{:S(2)}) async-start(bf16[8,4,160]{2,1,0:T(4,128)(2,1)} %copy.80), calls=%async_computation.3 | async-start | bytes 32768 | tf_op jit(solution)/shard_map/all_to_all | solution.py:131
  494.8 121.7 %all-to-all-start.1 = ((bf16[8,8,4,160,128]{4,3,2,1,0:T(8,128)(2,1)}), bf16[8,8,4,160,128]{4,3,2,1,0:T(8,128)(2,1)}, u32[]{:S(2)}, u32[]{:S(2)}) async-start(bf16[8,8,4,160,128]{4,3,2,1,0:T(8,128)(2,1)} %copy.78), calls=%async_computation.1 | async-start | bytes 20971520 | tf_op jit(solution)/shard_map/all_to_all | solution.py:117
  500.6 7.3 %slice-start = ((s8[8388608]{0:T(1024)(128)(4,1)}), s8[4194304]{0:T(1024)(128)(4,1)S(1)}, s32[]{:S(2)}) async-start(s8[8388608]{0:T(1024)(128)(4,1)} %bitcast.100), calls=%async_computation.5 | async-start | bytes 8388608
  504.8 3.1 slice-start.1
Sparse Core Ops, SparseCore 0:
  191.4 127.7 all-gather.1
